TPU v7x, 32 devices: a whole 2x2x4 slice. The times are simulated.
32 devices in a mesh: groups: 2 (over y), shard: 4 (over z), dp: 4 (over x, core).
Axes of the slice: x: 2, y: 2, z: 4, core: 2. Of those that a mesh axis runs over, the one named last changes fastest.
Arguments:
- maps_in: bfloat16 [32, 32, 1536], P(('groups', 'dp')), parts along dimension 0, may hold values from -6 to 6
- filters: bfloat16 [49, 1536], replicated, may hold values from -2 to 2
- w_expand: bfloat16 [1536, 6144], P(None, 'shard'), may hold values from -0.15625 to 0.15625
- w_project: bfloat16 [6144, 1536], P('shard'), may hold values from -0.078125 to 0.078125
- cotangent: bfloat16 [32, 32, 1536], P(('groups', 'dp')), parts along dimension 0, may hold values from -6 to 6
Outputs:
- block_out: bfloat16 [32, 32, 1536], P(('groups', 'dp')), parts along dimension 0
- grad_input: bfloat16 [32, 32, 1536], P(('groups', 'dp')), parts along dimension 0
- grad_expand: float32 [3072, 6144], P(('groups', 'dp'), 'shard'), parts along dimension 0
- grad_project: float32 [12288, 1536], P(('groups', 'shard'), 'dp'), parts along dimension 0
- grad_filters: float32 [98, 1536], P('groups'), parts along dimension 0
There are 2 independent parts, one for each index of `groups`. A program takes and returns all parts, laid end to end along the dimension named above; an argument that names none is the same for every part. Nothing has to cross between parts.
All inputs are finite; a program needn't handle non-finite values.
Results may differ from a plain program's by a relative error of at most 0.015.
Values may be sent and summed in bfloat16 or wider, within the bound.
A program may use at most 128 MiB of HBM per device.

v0:
```python
import jax
import jax.numpy as jnp
from jax import lax
from jax.sharding import PartitionSpec as P

KS = 7


def extended(block, sides, width):
    for axis, dim in sides:
        count = lax.axis_size(axis)
        forward = [(i, i + 1) for i in range(count - 1)]
        backward = [(target, source) for source, target in forward]
        low = lax.ppermute(
            lax.slice_in_dim(block, block.shape[dim] - width, None, axis=dim), axis, forward
        )
        high = lax.ppermute(lax.slice_in_dim(block, 0, width, axis=dim), axis, backward)
        block = jnp.concatenate([low, block, high], axis=dim)
    return block


def gelu_parts(hidden):
    cdf = 0.5 * (1.0 + jax.scipy.special.erf(hidden * 0.7071067811865476))
    density = jnp.exp(-0.5 * hidden * hidden) * 0.3989422804014327
    return (hidden * cdf, cdf + hidden * density)


def norm_stats(conv_rows):
    centered = conv_rows - jnp.mean(conv_rows, axis=-1, keepdims=True)
    variance = jnp.mean(centered * centered, axis=-1, keepdims=True)
    inv_scale = lax.rsqrt(variance + 1e-06)
    return (centered * inv_scale, inv_scale)


def norm_back(d_normed, scaled, inv_scale):
    first = jnp.mean(d_normed, axis=-1, keepdims=True)
    second = jnp.mean(d_normed * scaled, axis=-1, keepdims=True)
    return inv_scale * (d_normed - first - scaled * second)


def body(maps_in, filters, w_expand, w_project, cotangent):
    reach = KS // 2
    rows, cols, width = maps_in.shape
    count = rows * cols
    taps_f32 = filters.astype(jnp.float32)
    halo_in = extended(maps_in, (("dp", 0),), reach)
    padded_in = jnp.pad(halo_in, ((0, 0), (reach, reach), (0, 0)))
    conv_out = jnp.zeros((rows, cols, width), jnp.float32)
    for tap in range(KS * KS):
        tap_row, tap_col = divmod(tap, KS)
        conv_out = (
            conv_out
            + padded_in[tap_row : tap_row + rows, tap_col : tap_col + cols].astype(jnp.float32)
            * taps_f32[tap]
        )
    scaled, inv_scale = norm_stats(conv_out.reshape(count, width))
    normed = scaled.astype(jnp.bfloat16)
    hidden = jnp.dot(normed, w_expand, preferred_element_type=jnp.float32)
    activ, slope = gelu_parts(hidden)
    act = activ.astype(jnp.bfloat16)
    partial_out = jnp.dot(act, w_project, preferred_element_type=jnp.float32)
    cot_rows = cotangent.reshape(count, width)
    summed_out = lax.psum(partial_out.astype(jnp.bfloat16), "shard").astype(jnp.float32)
    d_act = lax.dot_general(
        cot_rows, w_project, (((1,), (1,)), ((), ())), preferred_element_type=jnp.float32
    )
    d_hidden = (d_act * slope).astype(jnp.bfloat16)
    grad_proj_local = lax.dot_general(
        act, cot_rows, (((0,), (0,)), ((), ())), preferred_element_type=jnp.float32
    )
    grad_exp_local = lax.dot_general(
        normed, d_hidden, (((0,), (0,)), ((), ())), preferred_element_type=jnp.float32
    )
    partial_norm = lax.dot_general(
        d_hidden, w_expand, (((1,), (1,)), ((), ())), preferred_element_type=jnp.float32
    )
    d_normed = lax.psum(partial_norm.astype(jnp.bfloat16), "shard").astype(jnp.float32)
    d_conv = norm_back(d_normed, scaled, inv_scale).astype(jnp.bfloat16)
    block_out = (
        (maps_in.reshape(count, width).astype(jnp.float32) + summed_out)
        .astype(jnp.bfloat16)
        .reshape(rows, cols, width)
    )
    grad_expand, grad_project = (
        lax.psum_scatter(
            grad_exp_local.astype(jnp.bfloat16), "dp", scatter_dimension=0, tiled=True
        ).astype(jnp.float32),
        lax.psum_scatter(
            grad_proj_local.astype(jnp.bfloat16), "dp", scatter_dimension=1, tiled=True
        ).astype(jnp.float32),
    )
    d_conv = d_conv.reshape(rows, cols, width)
    halo_grad = extended(d_conv, (("dp", 0),), reach)
    padded_grad = jnp.pad(halo_grad, ((0, 0), (reach, reach), (0, 0)))
    conv_grad = d_conv.astype(jnp.float32)
    back_sum = cotangent.astype(jnp.float32)
    filter_rows = []
    for tap in range(KS * KS):
        tap_row, tap_col = divmod(tap, KS)
        back_sum = (
            back_sum
            + padded_grad[
                2 * reach - tap_row : 2 * reach - tap_row + rows,
                2 * reach - tap_col : 2 * reach - tap_col + cols,
            ].astype(jnp.float32)
            * taps_f32[tap]
        )
        filter_rows.append(
            jnp.sum(
                conv_grad
                * padded_in[tap_row : tap_row + rows, tap_col : tap_col + cols].astype(jnp.float32),
                axis=(0, 1),
            )
        )
    grad_input = back_sum.astype(jnp.bfloat16)
    grad_filters = lax.psum(jnp.stack(filter_rows, axis=0).astype(jnp.bfloat16), "dp").astype(
        jnp.float32
    )
    return (block_out, grad_input, grad_expand, grad_project, grad_filters)


def solution(mesh):
    placed = (
        P(("groups", "dp"), None, None),
        P(),
        P(None, "shard"),
        P("shard", None),
        P(("groups", "dp"), None, None),
    )
    return jax.shard_map(
        body,
        mesh=mesh,
        in_specs=placed,
        out_specs=(
            P(("groups", "dp"), None, None),
            P(("groups", "dp"), None, None),
            P(("groups", "dp"), "shard"),
            P(("groups", "shard"), "dp"),
            P("groups", None),
        ),
        check_vma=False,
    )
```

profile of v0, /device:TPU:1, one launch (start us, length us, event | category | flops | bytes accessed | tf_op | source)
XLA Modules:
  0.0 244.2 jit_solution(9113310455872859118)
XLA Ops:
  8.4 4.5 %collective-permute-start = (bf16[3,32,1536]{2,1,0:T(8,128)(2,1)S(1)}, bf16[3,32,1536]{2,1,0:T(8,128)(2,1)S(1)}, u32[]{:S(2)}, u32[]{:S(2)}) collective-permute-start(bf16[3,32,1536]{2,1,0:T(8,128)(2,1)S(1)} %get-tuple-element.123), channel_id=1, source_target_pairs={{0,1},{1,2},{2,3},{4,5},{5,6},{6,7},{8,9},{9,10},{10,11},{12,13},{... | collective-permute-start | bytes 884744 | tf_op jit(solution)/shard_map/ppermute | solution.py:14
  12.9 1.9 collective-permute-start.1
  17.6 3.3 %collective-permute-done.1 = bf16[3,32,1536]{2,1,0:T(8,128)(2,1)S(1)} collective-permute-done((bf16[3,32,1536]{2,1,0:T(8,128)(2,1)S(1)}, bf16[3,32,1536]{2,1,0:T(8,128)(2,1)S(1)}, u32[]{:S(2)}, u32[]{:S(2)}) %collective-permute-start.1) | collective-permute-done | bytes 294944 | tf_op jit(solution)/shard_map/ppermute | solution.py:17
  21.5 9.2 %fusion.142 = (f32[4,32]{1,0:T(4,128)S(1)}, f32[4,32,1536]{2,1,0:T(8,128)S(1)}) fusion(f32[1536]{0:T(1024)S(1)} %get-tuple-element.66, bf16[10,38,1536]{2,1,0:T(8,128)(2,1)S(1)} %select_maximum_fusion.2, f32[1536]{0:T(1024)S(1)} %get-tuple-element.67, f32[1536]{0:T(1024)S(1)} %get-tuple-element.68, f32[1536]{0:T(1024)S(1)} %get-tuple-element.69, ...), kind=kLoop, calls=%fused_computation.326 | loop fusion | flops 28901248 | bytes 20355584 | tf_op jit(solution)/shard_map/reduce_sum | solution.py:29
  33.3 3.6 %fusion.146 = f32[128,1536]{1,0:T(8,128)S(1)} fusion(bf16[128,1536]{1,0:T(8,128)(2,1)S(1)} %fusion.136, bf16[1536,1536]{1,0:T(8,128)(2,1)} %param.7), kind=kOutput, calls=%fused_computation.329 | convolution fusion | flops 603979776 | bytes 5898240 | tf_op jit(solution)/shard_map/dot_general | solution.py:58
  36.9 4.2 %convolution_convert_fusion.3 = bf16[128,1536]{1,0:T(8,128)(2,1)} fusion(bf16[1536,1536]{1,0:T(8,128)(2,1)} %param.8, f32[128,1536]{1,0:T(8,128)S(1)} %fusion.146), kind=kOutput, calls=%fused_computation.57 | convolution fusion | flops 605159424 | bytes 5898240 | tf_op jit(solution)/shard_map/dot_general | solution.py:61
  41.2 1.6 fusion.1
  42.9 2.4 convolution_convert_fusion.2
  45.5 43.8 %all-reduce.8.cloned.1.call-done = (bf16[128,1536]{1,0:T(8,128)(2,1)}, bf16[128,1536]{1,0:T(8,128)(2,1)}) async-done(((bf16[128,1536]{1,0:T(8,128)(2,1)}, bf16[128,1536]{1,0:T(8,128)(2,1)}), (bf16[128,1536]{1,0:T(8,128)(2,1)}, bf16[128,1536]{1,0:T(8,128)(2,1)})) %all-reduce.8.cloned.1.call-update) | async-done | bytes 786448 | tf_op jit(solution)/shard_map/psum | solution.py:63
  90.7 3.5 %fusion.132 = (bf16[1536]{0:T(1024)(128)(2,1)S(1)}, bf16[1536]{0:T(1024)(128)(2,1)S(1)}, bf16[1536]{0:T(1024)(128)(2,1)S(1)}, bf16[1536]{0:T(1024)(128)(2,1)S(1)...) fusion(bf16[10,38,1536]{2,1,0:T(8,128)(2,1)S(1)} %select_maximu, ...), kind=kLoop, calls=%fused_computation.249 | loop fusion | flops 12358656 | bytes 8708096 | tf_op jit(solution)/shard_map/reduce_sum | solution.py:109
  95.4 2.0 fusion.111
  98.2 4.8 %stack.249 = bf16[49,1536]{1,0:T(8,128)(2,1)} concatenate(bf16[1,1536]{1,0:T(2,128)(2,1)S(1)} %stack.200, bf16[1,1536]{1,0:T(2,128)(2,1)S(1)} %stack.201, bf16[1,1536]{1,0:T(2,128)(2,1)S(1)} %stack.202, bf16[1,1536]{1,0:T(2,128)(2,1)S(1)} %stack.203, bf16[1,1536]{1,0:T(2,128)(2,1)S(1)} %stack.204, bf16[1,1536]{1,0:T(2,128)(2,1)S(1)} %stack.205, bf16[1,1536]{1,0:T(2,128)(2,1)S(1)} %stack.206, ...), dimensions={0} | concatenate | bytes 301056 | tf_op jit(solution)/shard_map/stack | solution.py:116
  103.0 3.6 %convolution_convert_fusion = bf16[1536,1536]{1,0:T(8,128)(2,1)} fusion(bf16[128,1536]{1,0:T(8,128)(2,1)S(1)} %bitcast.89, f32[128,1536]{1,0:T(8,128)S(1)} %copy-done.2), kind=kOutput, calls=%fused_computation.50 | convolution fusion | flops 607322112 | bytes 5898240 | tf_op jit(solution)/shard_map/dot_general | solution.py:68
  106.6 6.6 %copy.10 = bf16[1536,1536]{0,1:T(8,128)(2,1)} copy(bf16[1536,1536]{1,0:T(8,128)(2,1)} %convolution_convert_fusion) | data formatting | bytes 9437184
  114.4 3.6 %convolution_convert_fusion.1 = bf16[1536,1536]{1,0:T(8,128)(2,1)} fusion(bf16[128,1536]{1,0:T(8,128)(2,1)S(1)} %copy-done.6, bf16[128,1536]{1,0:T(8,128)(2,1)S(1)} %copy-done.10), kind=kOutput, calls=%fused_computation.51 | convolution fusion | flops 606339072 | bytes 5505024 | tf_op jit(solution)/shard_map/dot_general | solution.py:71
  118.4 3.8 %collective-permute-start.2 = (bf16[3,32,1536]{2,1,0:T(8,128)(2,1)S(1)}, bf16[3,32,1536]{2,1,0:T(8,128)(2,1)S(1)}, u32[]{:S(2)}, u32[]{:S(2)}) collective-permute-start(bf16[3,32,1536]{2,1,0:T(8,128)(2,1)S(1)} %bitcast.93), channel_id=1, source_target_pairs={{0,1},{1,2},{2,3},{4,5},{5,6},{6,7},{8,9},{9,10},{10,11},{12,13},{... | collective-permute-start | bytes 884744 | tf_op jit(solution)/shard_map/ppermute | solution.py:14
  122.2 1.9 collective-permute-start.3
  124.9 7.7 %all-reduce.6.cloned.1.call-done = bf16[49,1536]{1,0:T(8,128)(2,1)} async-done(((bf16[49,1536]{1,0:T(8,128)(2,1)}), bf16[49,1536]{1,0:T(8,128)(2,1)}) %all-reduce.6.cloned.1.call-update) | async-done | bytes 150544 | tf_op jit(solution)/shard_map/psum | solution.py:116
  132.7 1.7 convert_element_type.521
  135.1 7.4 %fusion.135 = bf16[4,32,1536]{2,1,0:T(8,128)(2,1)} fusion(bf16[4,32,1536]{2,1,0:T(8,128)(2,1)S(1)} %bitcast.85, bf16[4,32,1536]{2,1,0:T(8,128)(2,1)S(1)} %copy-done.8, bf16[3,32,1536]{2,1,0:T(8,128)(2,1)S(1)} %collective-permute-done.2, bf16[3,32,1536]{2,1,0:T(8,128)(2,1)S(1)} %collective-permute-done.3, bf16[10,38,1536]{2,1,0:T(8,128)(2,1)S(1)} %select_maximum_fusion, ...), kind=kLoop, calls=%fused_computation.257 | loop fusion | flops 30474240 | bytes 18585600 | tf_op jit(solution)/shard_map/convert_element_type | solution.py:115
  142.5 42.0 %reduce-scatter.7.cloned.1.call-done = bf16[384,1536]{1,0:T(8,128)(2,1)} async-done(((bf16[1536,1536]{1,0:T(8,128)(2,1)}), bf16[384,1536]{1,0:T(8,128)(2,1)}) %reduce-scatter.7.cloned.1.call-update) | async-done | bytes 1179664
  184.5 1.7 copy.11
  187.8 47.0 %reduce-scatter.5.cloned.1.call-done = bf16[384,1536]{1,0:T(8,128)(2,1)} async-done(((bf16[1536,1536]{1,0:T(8,128)(2,1)}), bf16[384,1536]{1,0:T(8,128)(2,1)}) %reduce-scatter.5.cloned.1.call-update) | async-done | bytes 1179664 | tf_op jit(solution)/shard_map/reduce_scatter | solution.py:85
  234.7 3.0 %convert_element_type.518 = f32[384,1536]{1,0:T(8,128)} convert(bf16[384,1536]{1,0:T(8,128)(2,1)} %reduce-scatter.5.cloned.1.call-done) | non-fusion elementwise | flops 589824 | bytes 3538944 | tf_op jit(solution)/shard_map/convert_element_type | solution.py:87
  (268 shorter events, 13.8 us)
Async XLA Ops:
  7.2 82.1 %all-reduce.8.cloned.1.call-start = ((), (), s32[]{:S(2)}) async-start(), calls=%async_computation.5 | async-start | bytes 1572864 | tf_op jit(solution)/shard_map/psum | solution.py:63
  8.4 9.1 %collective-permute-start = (bf16[3,32,1536]{2,1,0:T(8,128)(2,1)S(1)}, bf16[3,32,1536]{2,1,0:T(8,128)(2,1)S(1)}, u32[]{:S(2)}, u32[]{:S(2)}) collective-permute-start(bf16[3,32,1536]{2,1,0:T(8,128)(2,1)S(1)} %get-tuple-element.123), channel_id=1, source_target_pairs={{0,1},{1,2},{2,3},{4,5},{5,6},{6,7},{8,9},{9,10},{10,11},{12,13},{... | collective-permute-start | bytes 884744 | tf_op jit(solution)/shard_map/ppermute | solution.py:14
  12.9 8.0 %collective-permute-start.1 = (bf16[3,32,1536]{2,1,0:T(8,128)(2,1)S(1)}, bf16[3,32,1536]{2,1,0:T(8,128)(2,1)S(1)}, u32[]{:S(2)}, u32[]{:S(2)}) collective-permute-start(bf16[3,32,1536]{2,1,0:T(8,128)(2,1)S(1)} %get-tuple-element.124), channel_id=1, source_target_pairs={{1,0},{2,1},{3,2},{5,4},{6,5},{7,6},{9,8},{10,9},{11,10},{13,12},{... | collective-permute-start | bytes 884744 | tf_op jit(solution)/shard_map/ppermute | solution.py:17
  45.3 87.4 %all-reduce.6.cloned.1.call-start = ((), (), s32[]{:S(2)}) async-start(), calls=%async_computation.3 | async-start | bytes 344064 | tf_op jit(solution)/shard_map/psum | solution.py:116
  102.9 81.6 %reduce-scatter.7.cloned.1.call-start = ((), (), s32[]{:S(2)}) async-start(), calls=%async_computation.4 | async-start | bytes 5898240
  113.3 121.5 %reduce-scatter.5.cloned.1.call-start = ((), (), s32[]{:S(2)}) async-start(), calls=%async_computation.2 | async-start | bytes 5898240 | tf_op jit(solution)/shard_map/reduce_scatter | solution.py:85
  118.0 16.8 %copy-start.13 = (f32[1536]{0:T(1024)S(1)}, f32[1536]{0:T(1024)}, u32[]{:S(2)}) copy-start(f32[1536]{0:T(1024)} %copy-done.12) | copy-start | bytes 18436
  118.0 16.8 %copy-start.15 = (f32[1536]{0:T(1024)S(1)}, f32[1536]{0:T(1024)}, u32[]{:S(2)}) copy-start(f32[1536]{0:T(1024)} %copy-done.14) | copy-start | bytes 18436
  118.0 16.8 %copy-start.17 = (f32[1536]{0:T(1024)S(1)}, f32[1536]{0:T(1024)}, u32[]{:S(2)}) copy-start(f32[1536]{0:T(1024)} %copy-done.16) | copy-start | bytes 18436
  118.0 16.8 %copy-start.19 = (f32[1536]{0:T(1024)S(1)}, f32[1536]{0:T(1024)}, u32[]{:S(2)}) copy-start(f32[1536]{0:T(1024)} %copy-done.18) | copy-start | bytes 18436
  118.0 16.8 %copy-start.21 = (f32[1536]{0:T(1024)S(1)}, f32[1536]{0:T(1024)}, u32[]{:S(2)}) copy-start(f32[1536]{0:T(1024)} %copy-done.20) | copy-start | bytes 18436
  118.0 16.8 %copy-start.23 = (f32[1536]{0:T(1024)S(1)}, f32[1536]{0:T(1024)}, u32[]{:S(2)}) copy-start(f32[1536]{0:T(1024)} %copy-done.22) | copy-start | bytes 18436
  118.0 16.8 %copy-start.25 = (f32[1536]{0:T(1024)S(1)}, f32[1536]{0:T(1024)}, u32[]{:S(2)}) copy-start(f32[1536]{0:T(1024)} %copy-done.24) | copy-start | bytes 18436
  118.0 16.8 %copy-start.27 = (f32[1536]{0:T(1024)S(1)}, f32[1536]{0:T(1024)}, u32[]{:S(2)}) copy-start(f32[1536]{0:T(1024)} %copy-done.26) | copy-start | bytes 18436
  118.1 16.8 %copy-start.29 = (f32[1536]{0:T(1024)S(1)}, f32[1536]{0:T(1024)}, u32[]{:S(2)}) copy-start(f32[1536]{0:T(1024)} %copy-done.28) | copy-start | bytes 18436
  118.1 16.8 %copy-start.31 = (f32[1536]{0:T(1024)S(1)}, f32[1536]{0:T(1024)}, u32[]{:S(2)}) copy-start(f32[1536]{0:T(1024)} %copy-done.30) | copy-start | bytes 18436
  118.1 16.8 %copy-start.33 = (f32[1536]{0:T(1024)S(1)}, f32[1536]{0:T(1024)}, u32[]{:S(2)}) copy-start(f32[1536]{0:T(1024)} %copy-done.32) | copy-start | bytes 18436
  118.1 16.8 %copy-start.35 = (f32[1536]{0:T(1024)S(1)}, f32[1536]{0:T(1024)}, u32[]{:S(2)}) copy-start(f32[1536]{0:T(1024)} %copy-done.34) | copy-start | bytes 18436
  118.1 16.8 %copy-start.37 = (f32[1536]{0:T(1024)S(1)}, f32[1536]{0:T(1024)}, u32[]{:S(2)}) copy-start(f32[1536]{0:T(1024)} %copy-done.36) | copy-start | bytes 18436
  118.1 16.8 %copy-start.39 = (f32[1536]{0:T(1024)S(1)}, f32[1536]{0:T(1024)}, u32[]{:S(2)}) copy-start(f32[1536]{0:T(1024)} %copy-done.38) | copy-start | bytes 18436
  118.1 16.8 %copy-start.41 = (f32[1536]{0:T(1024)S(1)}, f32[1536]{0:T(1024)}, u32[]{:S(2)}) copy-start(f32[1536]{0:T(1024)} %copy-done.40) | copy-start | bytes 18436
  118.1 16.8 %copy-start.43 = (f32[1536]{0:T(1024)S(1)}, f32[1536]{0:T(1024)}, u32[]{:S(2)}) copy-start(f32[1536]{0:T(1024)} %copy-done.42) | copy-start | bytes 18436
  118.4 16.0 %collective-permute-start.2 = (bf16[3,32,1536]{2,1,0:T(8,128)(2,1)S(1)}, bf16[3,32,1536]{2,1,0:T(8,128)(2,1)S(1)}, u32[]{:S(2)}, u32[]{:S(2)}) collective-permute-start(bf16[3,32,1536]{2,1,0:T(8,128)(2,1)S(1)} %bitcast.93), channel_id=1, source_target_pairs={{0,1},{1,2},{2,3},{4,5},{5,6},{6,7},{8,9},{9,10},{10,11},{12,13},{... | collective-permute-start | bytes 884744 | tf_op jit(solution)/shard_map/ppermute | solution.py:14
  122.2 12.2 %collective-permute-start.3 = (bf16[3,32,1536]{2,1,0:T(8,128)(2,1)S(1)}, bf16[3,32,1536]{2,1,0:T(8,128)(2,1)S(1)}, u32[]{:S(2)}, u32[]{:S(2)}) collective-permute-start(bf16[3,32,1536]{2,1,0:T(8,128)(2,1)S(1)} %bitcast.92), channel_id=1, source_target_pairs={{1,0},{2,1},{3,2},{5,4},{6,5},{7,6},{9,8},{10,9},{11,10},{13,12},{... | collective-permute-start | bytes 884744 | tf_op jit(solution)/shard_map/ppermute | solution.py:17
  (76 other events, 792.0 us)
Sparse Core Ops, SparseCore 0:
  45.4 43.8 all-reduce.7
  103.1 29.5 all-reduce.5
  135.4 49.0 reduce-scatter.6
  186.9 47.8 reduce-scatter.4
where the time goes:
time: 245 us; the launch traced here: 244 us
  waiting for transfers between devices  144 us (59%)
  other arithmetic  34.5 us (14%)
  matrix products  19 us (8%)
  local copies, waits for them, and re-layouts  18.7 us (8%)
  between operations  15.7 us (6%)
  starting transfers between devices  12.4 us (5%)
    reduce_scatter x1, waiting for transfers between devices, body(): lax.psum_scatter(grad_exp_local.astype(jnp.bfloat16), 'dp', scatter_dimen...  47 us
    psum x1, waiting for transfers between devices, body(): lax.psum(partial_out.astype(jnp.bfloat16), 'shard').astype(jnp.float32)  43.8 us
    unnamed x5, waiting for transfers between devices  42.1 us
    unnamed x187, local copies, waits for them, and re-layouts  9.78 us
    reduce_sum x1, other arithmetic, norm_stats(): centered = conv_rows - jnp.mean(conv_rows, axis=-1, keepdims=True)  9.17 us
    ppermute x2, starting transfers between devices, extended(): lax.ppermute(lax.slice_in_dim(block, block.shape[dim] - width, None, axis...  8.26 us
    psum x1, waiting for transfers between devices, body(): lax.psum(jnp.stack(filter_rows, axis=0).astype(jnp.bfloat16), 'dp')  7.75 us
    convert_element_type x1, other arithmetic, body(): grad_input = back_sum.astype(jnp.bfloat16)  7.36 us
  transfers between devices with their start and end apart: 8, of which 5 were waited for; matrix products, arithmetic and copies ran while one was open for 12% of the time, Pallas kernels for 0%

commit v1 on v0

--- a/solution.py
+++ b/solution.py
@@ -1,9 +1,19 @@
+import functools
+
 import jax
 import jax.numpy as jnp
 from jax import lax
+from jax.experimental import pallas as pl
+from jax.experimental.pallas import tpu as pltpu
 from jax.sharding import PartitionSpec as P
 
 KS = 7
+REACH = KS // 2
+LANE = 128
+PAD = 8
+F32 = jnp.float32
+BF16 = jnp.bfloat16
+MESH = pl.DeviceIdType.MESH
 
 
 def extended(block, sides, width):
@@ -20,7 +30,7 @@
 
 
 def gelu_parts(hidden):
-    cdf = 0.5 * (1.0 + jax.scipy.special.erf(hidden * 0.7071067811865476))
+    cdf = 0.5 * (1.0 + lax.erf(hidden * 0.7071067811865476))
     density = jnp.exp(-0.5 * hidden * hidden) * 0.3989422804014327
     return (hidden * cdf, cdf + hidden * density)
 
@@ -38,7 +48,7 @@
     return inv_scale * (d_normed - first - scaled * second)
 
 
-def body(maps_in, filters, w_expand, w_project, cotangent):
+def plain_body(maps_in, filters, w_expand, w_project, cotangent):
     reach = KS // 2
     rows, cols, width = maps_in.shape
     count = rows * cols
@@ -119,6 +129,430 @@
     return (block_out, grad_input, grad_expand, grad_project, grad_filters)
 
 
+CONTRACT_LAST = (((1,), (1,)), ((), ()))
+CONTRACT_FIRST = (((0,), (0,)), ((), ()))
+
+
+def kernel(
+    S, R, W, C, H,
+    maps_ref, fil_ref, cot_ref, we_hbm, wp_hbm,
+    out_hbm, gin_hbm, ge_hbm, gp_hbm, gf_ref,
+    we, wp, fil, mp, halo_lo, halo_hi, conv, scaled, invs, dact,
+    nrm, cots, act, dh, ns, cs, pn, rn, po, ro, bo, st, rst,
+    dcv, dlo, dhi, dpad, fpart, fsum, fall, gi, ge, gp,
+    send, recv, loc,
+):
+    N = R * W
+    CH = C // S
+    DC = C // 4
+    g = lax.axis_index("groups")
+    s = lax.axis_index("shard")
+    d = lax.axis_index("dp")
+    pair_core = d + 1 - 2 * lax.rem(d, 2)
+    pair_chip = lax.rem(d + 2, 4)
+    peers = [lax.rem(s + k, S) for k in range(S)]
+    has_lo = d > 0
+    has_hi = d < 3
+
+    def chan(i):
+        return pl.ds(pl.multiple_of(i * CH, LANE), CH)
+
+    def dpcols(i):
+        return pl.ds(pl.multiple_of(i * DC, LANE), DC)
+
+    counter = [0]
+
+    def remote(src, dst, shard, dp):
+        i = counter[0]
+        counter[0] += 1
+        return pltpu.make_async_remote_copy(
+            src_ref=src, dst_ref=dst, send_sem=send.at[i], recv_sem=recv.at[i],
+            device_id=(g, shard, dp), device_id_type=MESH,
+        )
+
+    def move(src, dst, i):
+        return pltpu.make_async_copy(src, dst, loc.at[i])
+
+    cp_wp = move(wp_hbm, wp, 0)
+    cp_we = move(we_hbm, we, 1)
+    cp_wp.start()
+    cp_we.start()
+
+    barrier = pltpu.get_barrier_semaphore()
+    for k in range(1, S):
+        pl.semaphore_signal(barrier, inc=1, device_id=(g, peers[k], d), device_id_type=MESH)
+    for k in range(1, 4):
+        pl.semaphore_signal(
+            barrier, inc=1, device_id=(g, s, lax.rem(d + k, 4)), device_id_type=MESH
+        )
+    pl.semaphore_wait(barrier, S - 1 + 3)
+
+    lo_dp = jnp.maximum(d - 1, 0)
+    hi_dp = jnp.minimum(d + 1, 3)
+    to_hi = remote(maps_ref.at[pl.ds(R - REACH, REACH)], halo_lo, s, hi_dp)
+    to_lo = remote(maps_ref.at[pl.ds(0, REACH)], halo_hi, s, lo_dp)
+
+    @pl.when(has_hi)
+    def _():
+        to_hi.start()
+
+    @pl.when(has_lo)
+    def _():
+        to_lo.start()
+
+    c_cot = remote(cot_ref, cots, s, pair_chip)
+    c_cot.start()
+
+    fil[pl.ds(0, KS * KS), :] = fil_ref[...].astype(F32)
+    for r in range(R + 2 * REACH):
+        mp[r, pl.ds(0, PAD), :] = jnp.zeros((PAD, C), F32)
+        mp[r, pl.ds(PAD + W, PAD), :] = jnp.zeros((PAD, C), F32)
+        dpad[r, pl.ds(0, PAD), :] = jnp.zeros((PAD, CH), F32)
+        dpad[r, pl.ds(PAD + W, PAD), :] = jnp.zeros((PAD, CH), F32)
+    for r in range(R):
+        mp[REACH + r, pl.ds(PAD, W), :] = maps_ref[r].astype(F32)
+
+    HT = 256 if H % 256 == 0 else LANE
+    cp_wp.wait()
+
+    @pl.loop(0, H // HT)
+    def _(j):
+        o = pl.multiple_of(j * HT, HT)
+        dact[:, pl.ds(o, HT)] = lax.dot_general(
+            cot_ref[...], wp[pl.ds(o, HT), :], CONTRACT_LAST, preferred_element_type=F32
+        )
+
+    def fill(cond, copy, buf, target, base, width):
+        @pl.when(cond)
+        def _():
+            copy.wait_recv()
+            for r in range(REACH):
+                if len(buf.shape) == 3:
+                    target[base + r, pl.ds(PAD, W), :] = buf[r].astype(F32)
+                else:
+                    target[base + r, pl.ds(PAD, W), :] = buf[pl.ds(r * W, W), :].astype(F32)
+
+        @pl.when(jnp.logical_not(cond))
+        def _():
+            for r in range(REACH):
+                target[base + r, pl.ds(PAD, W), :] = jnp.zeros((W, width), F32)
+
+    fill(has_lo, to_hi, halo_lo, mp, 0, C)
+    fill(has_hi, to_lo, halo_hi, mp, REACH + R, C)
+
+    @pl.loop(0, C // LANE)
+    def _(t):
+        o = pl.ds(pl.multiple_of(t * LANE, LANE), LANE)
+        accs = [jnp.zeros((W, LANE), F32) for _ in range(R)]
+        for b in range(KS):
+            taps = [fil[pl.ds(a * KS + b, 1), o] for a in range(KS)]
+            for rin in range(R + 2 * REACH):
+                v = mp[rin, pl.ds(PAD - REACH + b, W), o]
+                for r in range(R):
+                    if 0 <= rin - r < KS:
+                        accs[r] = accs[r] + v * taps[rin - r]
+        for r in range(R):
+            conv[pl.ds(r * W, W), o] = accs[r]
+
+    @pl.loop(0, N // 16)
+    def _(t):
+        o = pl.ds(pl.multiple_of(t * 16, 16), 16)
+        sc, inv = norm_stats(conv[o, :])
+        scaled[o, :] = sc
+        invs[o, :] = jnp.broadcast_to(inv, (16, LANE))
+        nrm[0, o, :] = sc.astype(BF16)
+
+    c_nrm = remote(nrm.at[0], nrm.at[1], s, pair_chip)
+    c_nrm.start()
+
+    cp_we.wait()
+
+    @pl.loop(0, H // HT)
+    def _(j):
+        o = pl.ds(pl.multiple_of(j * HT, HT), HT)
+        hid = jnp.dot(nrm[0], we[:, o], preferred_element_type=F32)
+        a, slope = gelu_parts(hid)
+        act[0, :, o] = a.astype(BF16)
+        dh[0, :, o] = (dact[:, o] * slope).astype(BF16)
+
+    c_pn = []
+    for k in list(range(1, S)) + [0]:
+        t = peers[k]
+        pn[k] = lax.dot_general(
+            dh[0], we[chan(t), :], CONTRACT_LAST, preferred_element_type=F32
+        ).astype(BF16)
+        if k:
+            c = remote(pn.at[k], rn.at[k], t, d)
+            c.start()
+            c_pn.append(c)
+    c_po = []
+    for k in list(range(1, S)) + [0]:
+        t = peers[k]
+        po[k] = jnp.dot(act[0], wp[:, chan(t)], preferred_element_type=F32).astype(BF16)
+        if k:
+            c = remote(po.at[k], ro.at[k], t, d)
+            c.start()
+            c_po.append(c)
+
+    c_cot.wait_recv()
+    c_nrm.wait_recv()
+
+    @pl.loop(0, H // HT)
+    def _(j):
+        o = pl.ds(pl.multiple_of(j * HT, HT), HT)
+        hid = jnp.dot(nrm[1], we[:, o], preferred_element_type=F32)
+        da = lax.dot_general(
+            cots[...], wp[o, :], CONTRACT_LAST, preferred_element_type=F32
+        )
+        a, slope = gelu_parts(hid)
+        act[1, :, o] = a.astype(BF16)
+        dh[1, :, o] = (da * slope).astype(BF16)
+
+    pc = dpcols(pair_core)
+    mine = dpcols(d)
+    c_core = [
+        remote(act.at[pl.ds(0, 2)], act.at[pl.ds(2, 2)], s, pair_core),
+        remote(dh.at[pl.ds(0, 2)], dh.at[pl.ds(2, 2)], s, pair_core),
+        remote(nrm.at[pl.ds(0, 2), :, pc], ns.at[pl.ds(2, 2)], s, pair_core),
+        remote(cot_ref.at[:, pc], cs.at[2], s, pair_core),
+        remote(cots.at[:, pc], cs.at[3], s, pair_core),
+    ]
+    for c in c_core:
+        c.start()
+    ns[0] = nrm[0, :, mine]
+    ns[1] = nrm[1, :, mine]
+    cs[0] = cot_ref[:, mine]
+    cs[1] = cots[:, mine]
+
+    own = chan(s)
+    for c in c_pn:
+        c.wait_recv()
+    dn = pn[0].astype(F32)
+    for k in range(1, S):
+        dn = dn + rn[k].astype(F32)
+    sc = scaled[:, own]
+    first = jnp.sum(dn, axis=-1, keepdims=True)
+    second = jnp.sum(dn * sc, axis=-1, keepdims=True)
+    lane = lax.broadcasted_iota(jnp.int32, (N, LANE), 1)
+    st[...] = jnp.where(lane == 0, first, jnp.where(lane == 1, second, 0.0)).T[:8]
+    c_st = []
+    for k in range(1, S):
+        c = remote(st, rst.at[k], peers[k], d)
+        c.start()
+        c_st.append(c)
+    conv[:, pl.ds(0, CH)] = dn
+
+    for c in c_po:
+        c.wait_recv()
+    for r in range(R):
+        rows = pl.ds(r * W, W)
+        total = po[0, rows, :].astype(F32)
+        for k in range(1, S):
+            total = total + ro[k, rows, :].astype(F32)
+        bo[rows, :] = (mp[REACH + r, pl.ds(PAD, W), own] + total).astype(BF16)
+    c_bo = []
+    for k in range(1, S):
+        c = remote(bo, out_hbm.at[:, own], peers[k], d)
+        c.start()
+        c_bo.append(c)
+    l_bo = move(bo, out_hbm.at[:, own], 2)
+    l_bo.start()
+
+    for c in c_st:
+        c.wait_recv()
+    tot = st[...]
+    for k in range(1, S):
+        tot = tot + rst[k]
+    tot = jnp.concatenate([tot, jnp.zeros((LANE - 8, N), F32)], axis=0).T * (1.0 / C)
+    dcv[...] = (
+        invs[:, pl.ds(0, 1)]
+        * (conv[:, pl.ds(0, CH)] - tot[:, 0:1] - scaled[:, own] * tot[:, 1:2])
+    ).astype(BF16)
+    gto_hi = remote(dcv.at[pl.ds((R - REACH) * W, REACH * W)], dlo, s, hi_dp)
+    gto_lo = remote(dcv.at[pl.ds(0, REACH * W)], dhi, s, lo_dp)
+
+    @pl.when(has_hi)
+    def _():
+        gto_hi.start()
+
+    @pl.when(has_lo)
+    def _():
+        gto_lo.start()
+
+    for r in range(R):
+        dpad[REACH + r, pl.ds(PAD, W), :] = dcv[pl.ds(r * W, W), :].astype(F32)
+
+    fpart[...] = jnp.zeros_like(fpart)
+
+    @pl.loop(0, CH // LANE)
+    def _(t):
+        o = pl.ds(pl.multiple_of(t * LANE, LANE), LANE)
+        so = pl.ds(pl.multiple_of(s * CH + t * LANE, LANE), LANE)
+        grads = [dpad[REACH + r, pl.ds(PAD, W), o] for r in range(R)]
+        for b in range(KS):
+            sums = [jnp.zeros((W, LANE), F32) for _ in range(KS)]
+            for rin in range(R + 2 * REACH):
+                v = mp[rin, pl.ds(PAD - REACH + b, W), so]
+                for r in range(R):
+                    if 0 <= rin - r < KS:
+                        sums[rin - r] = sums[rin - r] + v * grads[r]
+            for a in range(KS):
+                fpart[pl.ds(a * KS + b, 1), o] = jnp.sum(sums[a], axis=0, keepdims=True)
+
+    fsum[d] = fpart[...].astype(BF16)
+    c_f = []
+    for k in range(1, 4):
+        c = remote(fsum.at[d], fsum.at[d], s, lax.rem(d + k, 4))
+        c.start()
+        c_f.append(c)
+
+    fill(has_lo, gto_hi, dlo, dpad, 0, CH)
+    fill(has_hi, gto_lo, dhi, dpad, REACH + R, CH)
+
+    @pl.loop(0, CH // LANE)
+    def _(t):
+        o = pl.ds(pl.multiple_of(t * LANE, LANE), LANE)
+        so = pl.ds(pl.multiple_of(s * CH + t * LANE, LANE), LANE)
+        accs = [cot_ref[pl.ds(r * W, W), so].astype(F32) for r in range(R)]
+        for b in range(KS):
+            taps = [fil[pl.ds(a * KS + b, 1), so] for a in range(KS)]
+            for rin in range(R + 2 * REACH):
+                v = dpad[rin, pl.ds(PAD + REACH - b, W), o]
+                for r in range(R):
+                    a = r + 2 * REACH - rin
+                    if 0 <= a < KS:
+                        accs[r] = accs[r] + v * taps[a]
+        for r in range(R):
+            gi[pl.ds(r * W, W), o] = accs[r].astype(BF16)
+
+    c_gi = []
+    for k in range(1, S):
+        c = remote(gi, gin_hbm.at[:, own], peers[k], d)
+        c.start()
+        c_gi.append(c)
+    l_gi = move(gi, gin_hbm.at[:, own], 3)
+    l_gi.start()
+
+    for c in c_f:
+        c.wait_recv()
+    fa = (fsum[0].astype(F32) + fsum[1].astype(F32)) + (
+        fsum[2].astype(F32) + fsum[3].astype(F32)
+    )
+    fall[s] = fa.astype(BF16)
+    c_fa = []
+    for k in range(1, S):
+        c = remote(fall.at[s], fall.at[s], peers[k], d)
+        c.start()
+        c_fa.append(c)
+
+    for c in c_core:
+        c.wait_recv()
+
+    @pl.loop(0, H // HT)
+    def _(j):
+        o = pl.ds(pl.multiple_of(j * HT, HT), HT)
+        ge[:, o] = lax.dot_general(
+            ns[...].reshape(4 * N, DC), dh[:, :, o].reshape(4 * N, HT),
+            CONTRACT_FIRST, preferred_element_type=F32,
+        )
+
+    l_ge = move(ge, ge_hbm, 4)
+    l_ge.start()
+
+    @pl.loop(0, H // HT)
+    def _(j):
+        o = pl.ds(pl.multiple_of(j * HT, HT), HT)
+        gp[o, :] = lax.dot_general(
+            act[:, :, o].reshape(4 * N, HT), cs[...].reshape(4 * N, DC),
+            CONTRACT_FIRST, preferred_element_type=F32,
+        )
+
+    l_gp = move(gp, gp_hbm, 5)
+    l_gp.start()
+
+    for c in c_fa:
+        c.wait_recv()
+    for t in range(S):
+        gf_ref[:, pl.ds(t * CH, CH)] = fall[t, pl.ds(0, KS * KS), :].astype(F32)
+    for c in c_bo + c_gi:
+        c.wait_recv()
+    for c in [c_cot, c_nrm] + c_pn + c_po + c_core + c_st + c_bo + c_f + c_gi + c_fa:
+        c.wait_send()
+    for c in (to_hi, gto_hi):
+        @pl.when(has_hi)
+        def _():
+            c.wait_send()
+    for c in (to_lo, gto_lo):
+        @pl.when(has_lo)
+        def _():
+            c.wait_send()
+    for c in (l_bo, l_gi, l_ge, l_gp):
+        c.wait()
+
+
+def kernel_body(maps_in, filters, w_expand, w_project, cotangent):
+    R, W, C = maps_in.shape
+    H = w_expand.shape[1]
+    S = lax.axis_size("shard")
+    N, CH, DC, RE = R * W, C // S, C // 4, R + 2 * REACH
+    VM = pltpu.VMEM
+    scratch = [
+        VM((C, H), BF16), VM((H, C), BF16), VM((56, C), F32),
+        VM((RE, W + 2 * PAD, C), F32),
+        VM((REACH, W, C), BF16), VM((REACH, W, C), BF16),
+        VM((N, C), F32), VM((N, C), F32), VM((N, LANE), F32), VM((N, H), F32),
+        VM((2, N, C), BF16), VM((N, C), BF16),
+        VM((4, N, H), BF16), VM((4, N, H), BF16),
+        VM((4, N, DC), BF16), VM((4, N, DC), BF16),
+        VM((S, N, CH), BF16), VM((S, N, CH), BF16),
+        VM((S, N, CH), BF16), VM((S, N, CH), BF16),
+        VM((N, CH), BF16), VM((8, N), F32), VM((S, 8, N), F32),
+        VM((N, CH), BF16), VM((REACH * W, CH), BF16), VM((REACH * W, CH), BF16),
+        VM((RE, W + 2 * PAD, CH), F32),
+        VM((64, CH), F32), VM((4, 64, CH), BF16), VM((S, 64, CH), BF16),
+        VM((N, CH), BF16), VM((DC, H), F32), VM((H, DC), F32),
+        pltpu.SemaphoreType.DMA((48,)), pltpu.SemaphoreType.DMA((48,)),
+        pltpu.SemaphoreType.DMA((8,)),
+    ]
+    vmem = pl.BlockSpec(memory_space=pltpu.VMEM)
+    anys = pl.BlockSpec(memory_space=pl.ANY)
+    out, gin, ge, gp, gf = pl.pallas_call(
+        functools.partial(kernel, S, R, W, C, H),
+        out_shape=(
+            jax.ShapeDtypeStruct((N, C), BF16),
+            jax.ShapeDtypeStruct((N, C), BF16),
+            jax.ShapeDtypeStruct((DC, H), F32),
+            jax.ShapeDtypeStruct((H, DC), F32),
+            jax.ShapeDtypeStruct((KS * KS, C), F32),
+        ),
+        in_specs=[vmem, vmem, vmem, anys, anys],
+        out_specs=(anys, anys, anys, anys, vmem),
+        scratch_shapes=scratch,
+        compiler_params=pltpu.CompilerParams(
+            collective_id=0, has_side_effects=True, vmem_limit_bytes=52 * 1024 * 1024
+        ),
+    )(maps_in, filters, cotangent.reshape(N, C), w_expand, w_project)
+    return (out.reshape(R, W, C), gin.reshape(R, W, C), ge, gp, gf)
+
+
+def body(maps_in, filters, w_expand, w_project, cotangent):
+    rows, cols, width = maps_in.shape
+    hid = w_expand.shape[1]
+    shards = lax.axis_size("shard")
+    fits = (
+        lax.axis_size("dp") == 4
+        and width % (shards * LANE) == 0
+        and width % (4 * LANE) == 0
+        and hid % LANE == 0
+        and shards > 1
+        and rows >= REACH
+        and rows * cols == LANE
+        and cols % 16 == 0
+    )
+    run = kernel_body if fits else plain_body
+    return run(maps_in, filters, w_expand, w_project, cotangent)
+
+
 def solution(mesh):
     placed = (
         P(("groups", "dp"), None, None),

time: 245 us -> 71 us (0.29)
  waiting for transfers between devices: 144 us -> 0 us
  Pallas kernels: 0 us -> 60.6 us
  other arithmetic: 34.5 us -> 0 us
  matrix products: 19 us -> 0 us
  between operations: 15.7 us -> 0.65 us
  starting transfers between devices: 12.4 us -> 0 us
  local copies, waits for them, and re-layouts: 18.7 us -> 8.91 us
    pallas_call x0 -> x1, Pallas kernels: none -> 60.6 us  [kernel_body(): pl.pallas_call(functools.partial(kernel, S, R, W, C, H), out_shape=(jax.S...]
    psum x2 -> x0, waiting for transfers between devices: 51.5 us -> none  [the longest x1 43.8 us: body(): lax.psum(partial_out.astype(jnp.bfloat16), 'shard').astype(jnp.float32)]
    reduce_scatter x1 -> x0, waiting for transfers between devices: 47 us -> none  [body(): lax.psum_scatter(grad_exp_local.astype(jnp.bfloat16), 'dp', scatter_dimen...]
    unnamed x5 -> x0, waiting for transfers between devices: 42.1 us -> none
    dot_general x6 -> x0, matrix products: 19 us -> none  [the longest x1 4.22 us: body(): partial_out = jnp.dot(act, w_project, preferred_element_type=jnp.float32)]
    reduce_sum x6 -> x0, other arithmetic: 17.5 us -> none  [the longest x1 9.17 us: norm_stats(): centered = conv_rows - jnp.mean(conv_rows, axis=-1, keepdims=True)]
    convert_element_type x7 -> x0, other arithmetic: 16.3 us -> none  [the longest x1 7.36 us: body(): grad_input = back_sum.astype(jnp.bfloat16)]
    ppermute x4 -> x0, starting transfers between devices: 12.1 us -> none  [the longest x2 8.26 us: extended(): lax.ppermute(lax.slice_in_dim(block, block.shape[dim] - width, None, axis...]
  transfers between devices with their start and end apart: 8 -> 0, of which waited for: 5 -> 0; matrix products, arithmetic and copies ran while one was open for 12% -> 0% of each run, Pallas kernels for 0% -> 0%
where the time goes in v1:
time: 71 us; the launch traced here: 70.1 us
  Pallas kernels  60.6 us (85%)
  local copies, waits for them, and re-layouts  8.91 us (13%)
    pallas_call x1, Pallas kernels, kernel_body(): pl.pallas_call(functools.partial(kernel, S, R, W, C, H), out_shape=(jax.S...  60.6 us
    unnamed x11, local copies, waits for them, and re-layouts  8.91 us

profile of v1, /device:TPU:1, one launch (start us, length us, event | category | flops | bytes accessed | tf_op | source)
XLA Modules:
  0.0 70.1 jit_solution(1575485372755728742)
XLA Ops:
  0.6 0.0 copy-start
  0.6 1.0 %copy-done = bf16[4,32,1536]{2,1,0:T(8,128)(2,1)S(1)} copy-done((bf16[4,32,1536]{2,1,0:T(8,128)(2,1)S(1)}, bf16[4,32,1536]{2,1,0:T(8,128)(2,1)}, u32[]{:S(2)}) %copy-start) | copy-done | bytes 393240
  1.6 0.0 copy-start.1
  1.6 0.9 %copy-done.1 = bf16[49,1536]{1,0:T(8,128)(2,1)S(1)} copy-done((bf16[49,1536]{1,0:T(8,128)(2,1)S(1)}, bf16[49,1536]{1,0:T(8,128)(2,1)}, u32[]{:S(2)}) %copy-start.1) | copy-done | bytes 150552
  2.5 60.6 %shard_map.92 = (bf16[128,1536]{1,0:T(8,128)(2,1)S(1)}, bf16[128,1536]{1,0:T(8,128)(2,1)S(1)}, f32[384,1536]{1,0:T(8,128)}, f32[1536,384]{1,0:T(8,128)}, f32[49,1536]{1,0:T(8,128)S(1)}) custom-call(bf16[4,32,1536]{2,1,0:T(8,128)(2,1)S(1)} %copy-done, bf16[49,1536]{1,0:T(8,128)(2,1)S(1)} %copy-done.1, bf16[128,1536]{1,0:T(8,128)(2,1)} %bitcast.5, ...), custom_call_target="tpu_custom_call" | custom-call | tf_op jit(solution)/shard_map/pallas_call | solution.py:519
  63.1 0.7 %copy.15 = bf16[4,32,1536]{2,1,0:T(8,128)(2,1)} copy(bf16[4,32,1536]{2,1,0:T(8,128)(2,1)S(1)} %bitcast.4) | data formatting | bytes 786432
  63.9 0.7 %copy.16 = bf16[4,32,1536]{2,1,0:T(8,128)(2,1)} copy(bf16[4,32,1536]{2,1,0:T(8,128)(2,1)S(1)} %bitcast.3) | data formatting | bytes 786432
  64.6 0.0 copy-start.2
  64.6 3.4 %copy.17 = f32[384,1536]{1,0:T(8,128)} copy(f32[384,1536]{1,0:T(8,128)} %get-tuple-element.22) | data formatting | bytes 4718592
  68.0 0.0 copy-done.2
  68.0 1.4 %copy.18 = f32[1536,384]{1,0:T(8,128)} copy(f32[1536,384]{1,0:T(8,128)S(1)} %copy-done.2) | data formatting | bytes 4718592
  69.4 0.7 %copy.19 = f32[49,1536]{1,0:T(8,128)} copy(f32[49,1536]{1,0:T(8,128)S(1)} %get-tuple-element.24) | data formatting | bytes 602112
Async XLA Ops:
  0.6 1.0 %copy-start = (bf16[4,32,1536]{2,1,0:T(8,128)(2,1)S(1)}, bf16[4,32,1536]{2,1,0:T(8,128)(2,1)}, u32[]{:S(2)}) copy-start(bf16[4,32,1536]{2,1,0:T(8,128)(2,1)} %maps_ref.1) | copy-start | bytes 1179652
  1.6 0.9 %copy-start.1 = (bf16[49,1536]{1,0:T(8,128)(2,1)S(1)}, bf16[49,1536]{1,0:T(8,128)(2,1)}, u32[]{:S(2)}) copy-start(bf16[49,1536]{1,0:T(8,128)(2,1)} %fil_ref.1) | copy-start | bytes 451588
  64.6 3.4 %copy-start.2 = (f32[1536,384]{1,0:T(8,128)S(1)}, f32[1536,384]{1,0:T(8,128)}, u32[]{:S(2)}) copy-start(f32[1536,384]{1,0:T(8,128)} %get-tuple-element.23) | copy-start | bytes 7077892

commit v2 on v1

--- a/solution.py
+++ b/solution.py
@@ -135,11 +135,11 @@
 
 def kernel(
     S, R, W, C, H,
-    maps_ref, fil_ref, cot_ref, we_hbm, wp_hbm,
-    out_hbm, gin_hbm, ge_hbm, gp_hbm, gf_ref,
-    we, wp, fil, mp, halo_lo, halo_hi, conv, scaled, invs, dact,
-    nrm, cots, act, dh, ns, cs, pn, rn, po, ro, bo, st, rst,
-    dcv, dlo, dhi, dpad, fpart, fsum, fall, gi, ge, gp,
+    maps_hbm, fil_hbm, cot_hbm, we_hbm, wp_hbm,
+    out_ref, gin_ref, ge, gp, gf_ref,
+    maps_ref, fil_ref, cot_ref, we, wp, fil, mp, halo_lo, halo_hi, conv, scaled, invs, dact,
+    nrm, cots, act, dh, ns, cs, pn, rn, po, ro, st, rst,
+    dcv, dlo, dhi, dpad, fpart, fsum, fall,
     send, recv, loc,
 ):
     N = R * W
@@ -175,6 +175,12 @@
 
     cp_wp = move(wp_hbm, wp, 0)
     cp_we = move(we_hbm, we, 1)
+    cp_maps = move(maps_hbm, maps_ref, 2)
+    cp_fil = move(fil_hbm, fil_ref, 3)
+    cp_cot = move(cot_hbm, cot_ref, 4)
+    cp_maps.start()
+    cp_cot.start()
+    cp_fil.start()
     cp_wp.start()
     cp_we.start()
 
@@ -189,8 +195,8 @@
 
     lo_dp = jnp.maximum(d - 1, 0)
     hi_dp = jnp.minimum(d + 1, 3)
-    to_hi = remote(maps_ref.at[pl.ds(R - REACH, REACH)], halo_lo, s, hi_dp)
-    to_lo = remote(maps_ref.at[pl.ds(0, REACH)], halo_hi, s, lo_dp)
+    to_hi = remote(maps_hbm.at[pl.ds(R - REACH, REACH)], halo_lo, s, hi_dp)
+    to_lo = remote(maps_hbm.at[pl.ds(0, REACH)], halo_hi, s, lo_dp)
 
     @pl.when(has_hi)
     def _():
@@ -200,9 +206,8 @@
     def _():
         to_lo.start()
 
-    c_cot = remote(cot_ref, cots, s, pair_chip)
-    c_cot.start()
-
+    cp_maps.wait()
+    cp_fil.wait()
     fil[pl.ds(0, KS * KS), :] = fil_ref[...].astype(F32)
     for r in range(R + 2 * REACH):
         mp[r, pl.ds(0, PAD), :] = jnp.zeros((PAD, C), F32)
@@ -213,6 +218,7 @@
         mp[REACH + r, pl.ds(PAD, W), :] = maps_ref[r].astype(F32)
 
     HT = 256 if H % 256 == 0 else LANE
+    cp_cot.wait()
     cp_wp.wait()
 
     @pl.loop(0, H // HT)
@@ -239,6 +245,8 @@
 
     fill(has_lo, to_hi, halo_lo, mp, 0, C)
     fill(has_hi, to_lo, halo_hi, mp, REACH + R, C)
+    c_cot = remote(cot_hbm, cots, s, pair_chip)
+    c_cot.start()
 
     @pl.loop(0, C // LANE)
     def _(t):
@@ -290,9 +298,7 @@
         t = peers[k]
         po[k] = jnp.dot(act[0], wp[:, chan(t)], preferred_element_type=F32).astype(BF16)
         if k:
-            c = remote(po.at[k], ro.at[k], t, d)
-            c.start()
-            c_po.append(c)
+            c_po.append(remote(po.at[k], ro.at[k], t, d))
 
     c_cot.wait_recv()
     c_nrm.wait_recv()
@@ -343,20 +349,7 @@
     conv[:, pl.ds(0, CH)] = dn
 
     for c in c_po:
-        c.wait_recv()
-    for r in range(R):
-        rows = pl.ds(r * W, W)
-        total = po[0, rows, :].astype(F32)
-        for k in range(1, S):
-            total = total + ro[k, rows, :].astype(F32)
-        bo[rows, :] = (mp[REACH + r, pl.ds(PAD, W), own] + total).astype(BF16)
-    c_bo = []
-    for k in range(1, S):
-        c = remote(bo, out_hbm.at[:, own], peers[k], d)
-        c.start()
-        c_bo.append(c)
-    l_bo = move(bo, out_hbm.at[:, own], 2)
-    l_bo.start()
+        c.start()
 
     for c in c_st:
         c.wait_recv()
@@ -423,15 +416,27 @@
                     if 0 <= a < KS:
                         accs[r] = accs[r] + v * taps[a]
         for r in range(R):
-            gi[pl.ds(r * W, W), o] = accs[r].astype(BF16)
+            gin_ref[pl.ds(r * W, W), so] = accs[r].astype(BF16)
 
     c_gi = []
     for k in range(1, S):
-        c = remote(gi, gin_hbm.at[:, own], peers[k], d)
+        c = remote(gin_ref.at[:, own], gin_ref.at[:, own], peers[k], d)
         c.start()
         c_gi.append(c)
-    l_gi = move(gi, gin_hbm.at[:, own], 3)
-    l_gi.start()
+
+    for c in c_po:
+        c.wait_recv()
+    for r in range(R):
+        rows = pl.ds(r * W, W)
+        total = po[0, rows, :].astype(F32)
+        for k in range(1, S):
+            total = total + ro[k, rows, :].astype(F32)
+        out_ref[rows, own] = (mp[REACH + r, pl.ds(PAD, W), own] + total).astype(BF16)
+    c_bo = []
+    for k in range(1, S):
+        c = remote(out_ref.at[:, own], out_ref.at[:, own], peers[k], d)
+        c.start()
+        c_bo.append(c)
 
     for c in c_f:
         c.wait_recv()
@@ -456,8 +461,6 @@
             CONTRACT_FIRST, preferred_element_type=F32,
         )
 
-    l_ge = move(ge, ge_hbm, 4)
-    l_ge.start()
 
     @pl.loop(0, H // HT)
     def _(j):
@@ -467,8 +470,6 @@
             CONTRACT_FIRST, preferred_element_type=F32,
         )
 
-    l_gp = move(gp, gp_hbm, 5)
-    l_gp.start()
 
     for c in c_fa:
         c.wait_recv()
@@ -486,7 +487,17 @@
         @pl.when(has_lo)
         def _():
             c.wait_send()
-    for c in (l_bo, l_gi, l_ge, l_gp):
+
+
+def store_kernel(*refs):
+    sems = refs[-1]
+    half = (len(refs) - 1) // 2
+    copies = [
+        pltpu.make_async_copy(refs[i], refs[half + i], sems.at[i]) for i in range(half)
+    ]
+    for c in copies:
+        c.start()
+    for c in copies:
         c.wait()
 
 
@@ -497,6 +508,7 @@
     N, CH, DC, RE = R * W, C // S, C // 4, R + 2 * REACH
     VM = pltpu.VMEM
     scratch = [
+        VM((R, W, C), BF16), VM((KS * KS, C), BF16), VM((N, C), BF16),
         VM((C, H), BF16), VM((H, C), BF16), VM((56, C), F32),
         VM((RE, W + 2 * PAD, C), F32),
         VM((REACH, W, C), BF16), VM((REACH, W, C), BF16),
@@ -506,32 +518,40 @@
         VM((4, N, DC), BF16), VM((4, N, DC), BF16),
         VM((S, N, CH), BF16), VM((S, N, CH), BF16),
         VM((S, N, CH), BF16), VM((S, N, CH), BF16),
-        VM((N, CH), BF16), VM((8, N), F32), VM((S, 8, N), F32),
+        VM((8, N), F32), VM((S, 8, N), F32),
         VM((N, CH), BF16), VM((REACH * W, CH), BF16), VM((REACH * W, CH), BF16),
         VM((RE, W + 2 * PAD, CH), F32),
         VM((64, CH), F32), VM((4, 64, CH), BF16), VM((S, 64, CH), BF16),
-        VM((N, CH), BF16), VM((DC, H), F32), VM((H, DC), F32),
         pltpu.SemaphoreType.DMA((48,)), pltpu.SemaphoreType.DMA((48,)),
         pltpu.SemaphoreType.DMA((8,)),
     ]
     vmem = pl.BlockSpec(memory_space=pltpu.VMEM)
     anys = pl.BlockSpec(memory_space=pl.ANY)
-    out, gin, ge, gp, gf = pl.pallas_call(
+    shapes = (
+        jax.ShapeDtypeStruct((N, C), BF16),
+        jax.ShapeDtypeStruct((N, C), BF16),
+        jax.ShapeDtypeStruct((DC, H), F32),
+        jax.ShapeDtypeStruct((H, DC), F32),
+        jax.ShapeDtypeStruct((KS * KS, C), F32),
+    )
+    results = pl.pallas_call(
         functools.partial(kernel, S, R, W, C, H),
-        out_shape=(
-            jax.ShapeDtypeStruct((N, C), BF16),
-            jax.ShapeDtypeStruct((N, C), BF16),
-            jax.ShapeDtypeStruct((DC, H), F32),
-            jax.ShapeDtypeStruct((H, DC), F32),
-            jax.ShapeDtypeStruct((KS * KS, C), F32),
-        ),
-        in_specs=[vmem, vmem, vmem, anys, anys],
-        out_specs=(anys, anys, anys, anys, vmem),
+        out_shape=shapes,
+        in_specs=[pl.BlockSpec(memory_space=pltpu.HBM)] * 5,
+        out_specs=(vmem,) * 5,
         scratch_shapes=scratch,
         compiler_params=pltpu.CompilerParams(
-            collective_id=0, has_side_effects=True, vmem_limit_bytes=52 * 1024 * 1024
+            collective_id=0, has_side_effects=True, vmem_limit_bytes=44 * 1024 * 1024
         ),
     )(maps_in, filters, cotangent.reshape(N, C), w_expand, w_project)
+    out, gin, ge, gp, gf = pl.pallas_call(
+        store_kernel,
+        out_shape=shapes,
+        in_specs=[anys] * 5,
+        out_specs=(anys,) * 5,
+        scratch_shapes=[pltpu.SemaphoreType.DMA((5,))],
+        compiler_params=pltpu.CompilerParams(vmem_limit_bytes=1024 * 1024),
+    )(*results)
     return (out.reshape(R, W, C), gin.reshape(R, W, C), ge, gp, gf)
 
 

time: 71 us -> 68.9 us (0.970)
  local copies, waits for them, and re-layouts: 8.91 us -> 2.9 us
  Pallas kernels: 60.6 us -> 64.2 us
    unnamed x11 -> x6, local copies, waits for them, and re-layouts: 8.91 us -> 2.9 us
    pallas_call x1 -> x2, Pallas kernels: 60.6 us -> 64.2 us  [the longest x1 61.6 us: kernel_body(): pl.pallas_call(functools.partial(kernel, S, R, W, C, H), out_shape=shapes...]
where the time goes in v2:
time: 68.9 us; the launch traced here: 67.7 us
  Pallas kernels  64.2 us (93%)
  local copies, waits for them, and re-layouts  2.9 us (4%)
    pallas_call x1, Pallas kernels, kernel_body(): pl.pallas_call(functools.partial(kernel, S, R, W, C, H), out_shape=shapes...  61.6 us
    unnamed x6, local copies, waits for them, and re-layouts  2.9 us
    pallas_call x1, Pallas kernels, kernel_body(): pl.pallas_call(store_kernel, out_shape=shapes, in_specs=[anys] * 5, out_s...  2.59 us

profile of v2, /device:TPU:1, one launch (start us, length us, event | category | flops | bytes accessed | tf_op | source)
XLA Modules:
  0.0 67.7 jit_solution(2970424643343473841)
XLA Ops:
  0.6 0.0 copy-start
  0.6 1.0 %copy-done = bf16[4,32,1536]{2,1,0:T(8,128)(2,1)S(1)} copy-done((bf16[4,32,1536]{2,1,0:T(8,128)(2,1)S(1)}, bf16[4,32,1536]{2,1,0:T(8,128)(2,1)}, u32[]{:S(2)}) %copy-start) | copy-done | bytes 393240
  1.6 0.0 copy-start.1
  1.6 1.0 %copy-done.1 = bf16[4,32,1536]{2,1,0:T(8,128)(2,1)S(1)} copy-done((bf16[4,32,1536]{2,1,0:T(8,128)(2,1)S(1)}, bf16[4,32,1536]{2,1,0:T(8,128)(2,1)}, u32[]{:S(2)}) %copy-start.1) | copy-done | bytes 393240
  2.6 0.0 copy-start.2
  2.6 0.9 %copy-done.2 = bf16[49,1536]{1,0:T(8,128)(2,1)S(1)} copy-done((bf16[49,1536]{1,0:T(8,128)(2,1)S(1)}, bf16[49,1536]{1,0:T(8,128)(2,1)}, u32[]{:S(2)}) %copy-start.2) | copy-done | bytes 150552
  3.5 61.6 %shard_map.92 = (bf16[128,1536]{1,0:T(8,128)(2,1)S(1)}, bf16[128,1536]{1,0:T(8,128)(2,1)S(1)}, f32[384,1536]{1,0:T(8,128)S(1)}, f32[1536,384]{1,0:T(8,128)S(1)}, f32[49,1536]{1,0:T(8,128)S(1)}) custom-call(bf16[4,32,1536]{2,1,0:T(8,128)(2,1)S(1)} %copy-done, bf16[49,1536]{1,0:T(8,128)(2,1)S(1)} %copy-done.2, bf16[128,1536]{1,0:T(8,128)(2,1)S(1)} %bitcast.3, ...), custom_call_target="tpu_custom_call" | custom-call | tf_op jit(solution)/shard_map/pallas_call | solution.py:537
  65.1 2.6 %shard_map.93 = (bf16[128,1536]{1,0:T(8,128)(2,1)}, bf16[128,1536]{1,0:T(8,128)(2,1)}, f32[384,1536]{1,0:T(8,128)}, f32[1536,384]{1,0:T(8,128)}, f32[49,1536]{1,0:T(8,128)}) custom-call(bf16[128,1536]{1,0:T(8,128)(2,1)S(1)} %get-tuple-element.15.refs_0_, bf16[128,1536]{1,0:T(8,128)(2,1)S(1)} %get-tuple-element.16.refs_1_, ...), custom_call_target="tpu_custom_call" | custom-call | tf_op jit(solution)/shard_map/pallas_call | solution.py:547
Async XLA Ops:
  0.6 1.0 %copy-start = (bf16[4,32,1536]{2,1,0:T(8,128)(2,1)S(1)}, bf16[4,32,1536]{2,1,0:T(8,128)(2,1)}, u32[]{:S(2)}) copy-start(bf16[4,32,1536]{2,1,0:T(8,128)(2,1)} %maps_hbm.1) | copy-start | bytes 1179652
  1.6 1.0 %copy-start.1 = (bf16[4,32,1536]{2,1,0:T(8,128)(2,1)S(1)}, bf16[4,32,1536]{2,1,0:T(8,128)(2,1)}, u32[]{:S(2)}) copy-start(bf16[4,32,1536]{2,1,0:T(8,128)(2,1)} %param.9) | copy-start | bytes 1179652
  2.6 0.9 %copy-start.2 = (bf16[49,1536]{1,0:T(8,128)(2,1)S(1)}, bf16[49,1536]{1,0:T(8,128)(2,1)}, u32[]{:S(2)}) copy-start(bf16[49,1536]{1,0:T(8,128)(2,1)} %fil_hbm.1) | copy-start | bytes 451588

commit v3 on v2

--- a/solution.py
+++ b/solution.py
@@ -139,7 +139,7 @@
     out_ref, gin_ref, ge, gp, gf_ref,
     maps_ref, fil_ref, cot_ref, we, wp, fil, mp, halo_lo, halo_hi, conv, scaled, invs, dact,
     nrm, cots, act, dh, ns, cs, pn, rn, po, ro, st, rst,
-    dcv, dlo, dhi, dpad, fpart, fsum, fall,
+    dcv, dlo, dhi, dpad, fpart, fsend, fsum, fall,
     send, recv, loc,
 ):
     N = R * W
@@ -301,34 +301,13 @@
             c_po.append(remote(po.at[k], ro.at[k], t, d))
 
     c_cot.wait_recv()
-    c_nrm.wait_recv()
 
     @pl.loop(0, H // HT)
     def _(j):
-        o = pl.ds(pl.multiple_of(j * HT, HT), HT)
-        hid = jnp.dot(nrm[1], we[:, o], preferred_element_type=F32)
-        da = lax.dot_general(
-            cots[...], wp[o, :], CONTRACT_LAST, preferred_element_type=F32
-        )
-        a, slope = gelu_parts(hid)
-        act[1, :, o] = a.astype(BF16)
-        dh[1, :, o] = (da * slope).astype(BF16)
-
-    pc = dpcols(pair_core)
-    mine = dpcols(d)
-    c_core = [
-        remote(act.at[pl.ds(0, 2)], act.at[pl.ds(2, 2)], s, pair_core),
-        remote(dh.at[pl.ds(0, 2)], dh.at[pl.ds(2, 2)], s, pair_core),
-        remote(nrm.at[pl.ds(0, 2), :, pc], ns.at[pl.ds(2, 2)], s, pair_core),
-        remote(cot_ref.at[:, pc], cs.at[2], s, pair_core),
-        remote(cots.at[:, pc], cs.at[3], s, pair_core),
-    ]
-    for c in c_core:
-        c.start()
-    ns[0] = nrm[0, :, mine]
-    ns[1] = nrm[1, :, mine]
-    cs[0] = cot_ref[:, mine]
-    cs[1] = cots[:, mine]
+        o = pl.multiple_of(j * HT, HT)
+        dact[:, pl.ds(o, HT)] = lax.dot_general(
+            cots[...], wp[pl.ds(o, HT), :], CONTRACT_LAST, preferred_element_type=F32
+        )
 
     own = chan(s)
     for c in c_pn:
@@ -392,10 +371,14 @@
             for a in range(KS):
                 fpart[pl.ds(a * KS + b, 1), o] = jnp.sum(sums[a], axis=0, keepdims=True)
 
-    fsum[d] = fpart[...].astype(BF16)
+    fsend[...] = fpart[...].astype(BF16)
+    fsum[d] = fsend[pl.ds(pl.multiple_of(d * 16, 16), 16), :]
     c_f = []
     for k in range(1, 4):
-        c = remote(fsum.at[d], fsum.at[d], s, lax.rem(d + k, 4))
+        t = lax.rem(d + k, 4)
+        c = remote(
+            fsend.at[pl.ds(pl.multiple_of(t * 16, 16), 16)], fsum.at[d], s, t
+        )
         c.start()
         c_f.append(c)
 
@@ -424,6 +407,18 @@
         c.start()
         c_gi.append(c)
 
+    for c in c_f:
+        c.wait_recv()
+    fa = (fsum[0].astype(F32) + fsum[1].astype(F32)) + (
+        fsum[2].astype(F32) + fsum[3].astype(F32)
+    )
+    fall[d, s] = fa.astype(BF16)
+    c_fz = []
+    for k in range(1, S):
+        c = remote(fall.at[d, s], fall.at[d, s], peers[k], d)
+        c.start()
+        c_fz.append(c)
+
     for c in c_po:
         c.wait_recv()
     for r in range(R):
@@ -438,15 +433,37 @@
         c.start()
         c_bo.append(c)
 
-    for c in c_f:
-        c.wait_recv()
-    fa = (fsum[0].astype(F32) + fsum[1].astype(F32)) + (
-        fsum[2].astype(F32) + fsum[3].astype(F32)
-    )
-    fall[s] = fa.astype(BF16)
+    c_nrm.wait_recv()
+
+    @pl.loop(0, H // HT)
+    def _(j):
+        o = pl.ds(pl.multiple_of(j * HT, HT), HT)
+        hid = jnp.dot(nrm[1], we[:, o], preferred_element_type=F32)
+        a, slope = gelu_parts(hid)
+        act[1, :, o] = a.astype(BF16)
+        dh[1, :, o] = (dact[:, o] * slope).astype(BF16)
+
+    pc = dpcols(pair_core)
+    mine = dpcols(d)
+    c_core = [
+        remote(act.at[pl.ds(0, 2)], act.at[pl.ds(2, 2)], s, pair_core),
+        remote(dh.at[pl.ds(0, 2)], dh.at[pl.ds(2, 2)], s, pair_core),
+        remote(nrm.at[pl.ds(0, 2), :, pc], ns.at[pl.ds(2, 2)], s, pair_core),
+        remote(cot_ref.at[:, pc], cs.at[2], s, pair_core),
+        remote(cots.at[:, pc], cs.at[3], s, pair_core),
+    ]
+    for c in c_core:
+        c.start()
+    ns[0] = nrm[0, :, mine]
+    ns[1] = nrm[1, :, mine]
+    cs[0] = cot_ref[:, mine]
+    cs[1] = cots[:, mine]
+
+    for c in c_fz:
+        c.wait_recv()
     c_fa = []
-    for k in range(1, S):
-        c = remote(fall.at[s], fall.at[s], peers[k], d)
+    for k in range(1, 4):
+        c = remote(fall.at[d], fall.at[d], s, lax.rem(d + k, 4))
         c.start()
         c_fa.append(c)
 
@@ -473,11 +490,13 @@
 
     for c in c_fa:
         c.wait_recv()
-    for t in range(S):
-        gf_ref[:, pl.ds(t * CH, CH)] = fall[t, pl.ds(0, KS * KS), :].astype(F32)
+    for q in range(4):
+        n = min(16, KS * KS - 16 * q)
+        for t in range(S):
+            gf_ref[pl.ds(16 * q, n), pl.ds(t * CH, CH)] = fall[q, t].astype(F32)[:n]
     for c in c_bo + c_gi:
         c.wait_recv()
-    for c in [c_cot, c_nrm] + c_pn + c_po + c_core + c_st + c_bo + c_f + c_gi + c_fa:
+    for c in [c_cot, c_nrm] + c_pn + c_po + c_core + c_st + c_bo + c_f + c_fz + c_gi + c_fa:
         c.wait_send()
     for c in (to_hi, gto_hi):
         @pl.when(has_hi)
@@ -521,7 +540,7 @@
         VM((8, N), F32), VM((S, 8, N), F32),
         VM((N, CH), BF16), VM((REACH * W, CH), BF16), VM((REACH * W, CH), BF16),
         VM((RE, W + 2 * PAD, CH), F32),
-        VM((64, CH), F32), VM((4, 64, CH), BF16), VM((S, 64, CH), BF16),
+        VM((64, CH), F32), VM((64, CH), BF16), VM((4, 16, CH), BF16), VM((4, S, 16, CH), BF16),
         pltpu.SemaphoreType.DMA((48,)), pltpu.SemaphoreType.DMA((48,)),
         pltpu.SemaphoreType.DMA((8,)),
     ]

time: 68.9 us -> 68.4 us (level); the launches traced: 67.7 us -> 68.2 us
  no operation moved by 1% of the time
where the time goes in v3:
time: 68.4 us; the launch traced here: 68.2 us
  Pallas kernels  64.6 us (94%)
  local copies, waits for them, and re-layouts  2.9 us (4%)
    pallas_call x1, Pallas kernels, kernel_body(): pl.pallas_call(functools.partial(kernel, S, R, W, C, H), out_shape=shapes...  62 us
    unnamed x6, local copies, waits for them, and re-layouts  2.9 us
    pallas_call x1, Pallas kernels, kernel_body(): pl.pallas_call(store_kernel, out_shape=shapes, in_specs=[anys] * 5, out_s...  2.59 us

profile of v3, /device:TPU:1, one launch (start us, length us, event | category | flops | bytes accessed | tf_op | source)
XLA Modules:
  0.0 68.2 jit_solution(5641467848887008051)
XLA Ops:
  0.6 0.0 copy-start
  0.6 1.0 %copy-done = bf16[4,32,1536]{2,1,0:T(8,128)(2,1)S(1)} copy-done((bf16[4,32,1536]{2,1,0:T(8,128)(2,1)S(1)}, bf16[4,32,1536]{2,1,0:T(8,128)(2,1)}, u32[]{:S(2)}) %copy-start) | copy-done | bytes 393240
  1.6 0.0 copy-start.1
  1.6 1.0 %copy-done.1 = bf16[4,32,1536]{2,1,0:T(8,128)(2,1)S(1)} copy-done((bf16[4,32,1536]{2,1,0:T(8,128)(2,1)S(1)}, bf16[4,32,1536]{2,1,0:T(8,128)(2,1)}, u32[]{:S(2)}) %copy-start.1) | copy-done | bytes 393240
  2.6 0.0 copy-start.2
  2.6 0.9 %copy-done.2 = bf16[49,1536]{1,0:T(8,128)(2,1)S(1)} copy-done((bf16[49,1536]{1,0:T(8,128)(2,1)S(1)}, bf16[49,1536]{1,0:T(8,128)(2,1)}, u32[]{:S(2)}) %copy-start.2) | copy-done | bytes 150552
  3.5 62.0 %shard_map.92 = (bf16[128,1536]{1,0:T(8,128)(2,1)S(1)}, bf16[128,1536]{1,0:T(8,128)(2,1)S(1)}, f32[384,1536]{1,0:T(8,128)S(1)}, f32[1536,384]{1,0:T(8,128)S(1)}, f32[49,1536]{1,0:T(8,128)S(1)}) custom-call(bf16[4,32,1536]{2,1,0:T(8,128)(2,1)S(1)} %copy-done, bf16[49,1536]{1,0:T(8,128)(2,1)S(1)} %copy-done.2, bf16[128,1536]{1,0:T(8,128)(2,1)S(1)} %bitcast.3, ...), custom_call_target="tpu_custom_call" | custom-call | tf_op jit(solution)/shard_map/pallas_call | solution.py:556
  65.6 2.6 %shard_map.93 = (bf16[128,1536]{1,0:T(8,128)(2,1)}, bf16[128,1536]{1,0:T(8,128)(2,1)}, f32[384,1536]{1,0:T(8,128)}, f32[1536,384]{1,0:T(8,128)}, f32[49,1536]{1,0:T(8,128)}) custom-call(bf16[128,1536]{1,0:T(8,128)(2,1)S(1)} %get-tuple-element.15.refs_0_, bf16[128,1536]{1,0:T(8,128)(2,1)S(1)} %get-tuple-element.16.refs_1_, ...), custom_call_target="tpu_custom_call" | custom-call | tf_op jit(solution)/shard_map/pallas_call | solution.py:566
Async XLA Ops:
  0.6 1.0 %copy-start = (bf16[4,32,1536]{2,1,0:T(8,128)(2,1)S(1)}, bf16[4,32,1536]{2,1,0:T(8,128)(2,1)}, u32[]{:S(2)}) copy-start(bf16[4,32,1536]{2,1,0:T(8,128)(2,1)} %maps_hbm.1) | copy-start | bytes 1179652
  1.6 1.0 %copy-start.1 = (bf16[4,32,1536]{2,1,0:T(8,128)(2,1)S(1)}, bf16[4,32,1536]{2,1,0:T(8,128)(2,1)}, u32[]{:S(2)}) copy-start(bf16[4,32,1536]{2,1,0:T(8,128)(2,1)} %param.9) | copy-start | bytes 1179652
  2.6 0.9 %copy-start.2 = (bf16[49,1536]{1,0:T(8,128)(2,1)S(1)}, bf16[49,1536]{1,0:T(8,128)(2,1)}, u32[]{:S(2)}) copy-start(bf16[49,1536]{1,0:T(8,128)(2,1)} %fil_hbm.1) | copy-start | bytes 451588

commit v4 on v3

--- a/solution.py
+++ b/solution.py
@@ -300,15 +300,6 @@
         if k:
             c_po.append(remote(po.at[k], ro.at[k], t, d))
 
-    c_cot.wait_recv()
-
-    @pl.loop(0, H // HT)
-    def _(j):
-        o = pl.multiple_of(j * HT, HT)
-        dact[:, pl.ds(o, HT)] = lax.dot_general(
-            cots[...], wp[pl.ds(o, HT), :], CONTRACT_LAST, preferred_element_type=F32
-        )
-
     own = chan(s)
     for c in c_pn:
         c.wait_recv()
@@ -433,6 +424,7 @@
         c.start()
         c_bo.append(c)
 
+    c_cot.wait_recv()
     c_nrm.wait_recv()
 
     @pl.loop(0, H // HT)
@@ -441,7 +433,10 @@
         hid = jnp.dot(nrm[1], we[:, o], preferred_element_type=F32)
         a, slope = gelu_parts(hid)
         act[1, :, o] = a.astype(BF16)
-        dh[1, :, o] = (dact[:, o] * slope).astype(BF16)
+        da = lax.dot_general(
+            cots[...], wp[o, :], CONTRACT_LAST, preferred_element_type=F32
+        )
+        dh[1, :, o] = (da * slope).astype(BF16)
 
     pc = dpcols(pair_core)
     mine = dpcols(d)

time: 68.4 us -> 68.4 us (level)
  no operation moved by 1% of the time
where the time goes in v4:
time: 68.4 us; the launch traced here: 68.2 us
  Pallas kernels  64.6 us (94%)
  local copies, waits for them, and re-layouts  2.9 us (4%)
    pallas_call x1, Pallas kernels, kernel_body(): pl.pallas_call(functools.partial(kernel, S, R, W, C, H), out_shape=shapes...  62 us
    unnamed x6, local copies, waits for them, and re-layouts  2.9 us
    pallas_call x1, Pallas kernels, kernel_body(): pl.pallas_call(store_kernel, out_shape=shapes, in_specs=[anys] * 5, out_s...  2.59 us

profile of v4, /device:TPU:1, one launch (start us, length us, event | category | flops | bytes accessed | tf_op | source)
XLA Modules:
  0.0 68.2 jit_solution(17236738773257861942)
XLA Ops:
  0.6 0.0 copy-start
  0.6 1.0 %copy-done = bf16[4,32,1536]{2,1,0:T(8,128)(2,1)S(1)} copy-done((bf16[4,32,1536]{2,1,0:T(8,128)(2,1)S(1)}, bf16[4,32,1536]{2,1,0:T(8,128)(2,1)}, u32[]{:S(2)}) %copy-start) | copy-done | bytes 393240
  1.6 0.0 copy-start.1
  1.6 1.0 %copy-done.1 = bf16[4,32,1536]{2,1,0:T(8,128)(2,1)S(1)} copy-done((bf16[4,32,1536]{2,1,0:T(8,128)(2,1)S(1)}, bf16[4,32,1536]{2,1,0:T(8,128)(2,1)}, u32[]{:S(2)}) %copy-start.1) | copy-done | bytes 393240
  2.6 0.0 copy-start.2
  2.6 0.9 %copy-done.2 = bf16[49,1536]{1,0:T(8,128)(2,1)S(1)} copy-done((bf16[49,1536]{1,0:T(8,128)(2,1)S(1)}, bf16[49,1536]{1,0:T(8,128)(2,1)}, u32[]{:S(2)}) %copy-start.2) | copy-done | bytes 150552
  3.5 62.0 %shard_map.92 = (bf16[128,1536]{1,0:T(8,128)(2,1)S(1)}, bf16[128,1536]{1,0:T(8,128)(2,1)S(1)}, f32[384,1536]{1,0:T(8,128)S(1)}, f32[1536,384]{1,0:T(8,128)S(1)}, f32[49,1536]{1,0:T(8,128)S(1)}) custom-call(bf16[4,32,1536]{2,1,0:T(8,128)(2,1)S(1)} %copy-done, bf16[49,1536]{1,0:T(8,128)(2,1)S(1)} %copy-done.2, bf16[128,1536]{1,0:T(8,128)(2,1)S(1)} %bitcast.3, ...), custom_call_target="tpu_custom_call" | custom-call | tf_op jit(solution)/shard_map/pallas_call | solution.py:551
  65.6 2.6 %shard_map.93 = (bf16[128,1536]{1,0:T(8,128)(2,1)}, bf16[128,1536]{1,0:T(8,128)(2,1)}, f32[384,1536]{1,0:T(8,128)}, f32[1536,384]{1,0:T(8,128)}, f32[49,1536]{1,0:T(8,128)}) custom-call(bf16[128,1536]{1,0:T(8,128)(2,1)S(1)} %get-tuple-element.15.refs_0_, bf16[128,1536]{1,0:T(8,128)(2,1)S(1)} %get-tuple-element.16.refs_1_, ...), custom_call_target="tpu_custom_call" | custom-call | tf_op jit(solution)/shard_map/pallas_call | solution.py:561
Async XLA Ops:
  0.6 1.0 %copy-start = (bf16[4,32,1536]{2,1,0:T(8,128)(2,1)S(1)}, bf16[4,32,1536]{2,1,0:T(8,128)(2,1)}, u32[]{:S(2)}) copy-start(bf16[4,32,1536]{2,1,0:T(8,128)(2,1)} %maps_hbm.1) | copy-start | bytes 1179652
  1.6 1.0 %copy-start.1 = (bf16[4,32,1536]{2,1,0:T(8,128)(2,1)S(1)}, bf16[4,32,1536]{2,1,0:T(8,128)(2,1)}, u32[]{:S(2)}) copy-start(bf16[4,32,1536]{2,1,0:T(8,128)(2,1)} %param.9) | copy-start | bytes 1179652
  2.6 0.9 %copy-start.2 = (bf16[49,1536]{1,0:T(8,128)(2,1)S(1)}, bf16[49,1536]{1,0:T(8,128)(2,1)}, u32[]{:S(2)}) copy-start(bf16[49,1536]{1,0:T(8,128)(2,1)} %fil_hbm.1) | copy-start | bytes 451588
